TPU v7x, 128 devices: a whole 4x4x4 slice. The times are simulated.
128 devices in a mesh: dp: 16 (over x_lo, z, core), tensor: 8 (over y, x_hi).
Axes of the slice: x: 4 (x_hi: 2, x_lo: 2; x = x_hi * 2 + x_lo), y: 4, z: 4, core: 2. Of those that a mesh axis runs over, the one named last changes fastest.
Arguments:
- tokens: bfloat16 [16384, 2048], P(('dp', 'tensor')), may hold values from -6 to 6
- cotangent: bfloat16 [16384, 2048], P(('dp', 'tensor')), may hold values from -6 to 6
- attn_gain: float32 [2048], replicated, may hold values from 0.1 to 1.9
- mlp_gain: float32 [2048], replicated, may hold values from 0.1 to 1.9
- query_gain: float32 [128], replicated, may hold values from 0.1 to 1.9
- key_gain: float32 [128], replicated, may hold values from 0.1 to 1.9
- w_query: bfloat16 [2048, 2048], P('dp', 'tensor'), may hold values from -0.125 to 0.125
- key_weight: bfloat16 [2048, 1024], P('dp', 'tensor'), may hold values from -0.125 to 0.125
- value_weight: bfloat16 [2048, 1024], P('dp', 'tensor'), may hold values from -0.125 to 0.125
- w_out: bfloat16 [2048, 2048], P('dp', 'tensor'), may hold values from -1.5 to 1.5
- w_gate: bfloat16 [2048, 6144], P('dp', 'tensor'), may hold values from -0.125 to 0.125
- w_up: bfloat16 [2048, 6144], P('dp', 'tensor'), may hold values from -0.125 to 0.125
- w_down: bfloat16 [2048, 6144], P('dp', 'tensor'), may hold values from -0.078125 to 0.078125
Outputs:
- result: bfloat16 [16384, 2048], P(('dp', 'tensor'))
- tokens_grad: float32 [16384, 2048], P(('dp', 'tensor'))
- attn_gain_grad: float32 [2048], replicated
- mlp_gain_grad: float32 [2048], replicated
- query_gain_grad: float32 [128], replicated
- key_gain_grad: float32 [128], replicated
- w_query_grad: float32 [2048, 2048], P('dp', 'tensor')
- key_weight_gradient: float32 [2048, 1024], P('dp', 'tensor')
- w_value_grad: float32 [2048, 1024], P('dp', 'tensor')
- w_out_grad: float32 [2048, 2048], P('dp', 'tensor')
- w_gate_grad: float32 [2048, 6144], P('dp', 'tensor')
- w_up_grad: float32 [2048, 6144], P('dp', 'tensor')
- w_down_grad: float32 [2048, 6144], P('dp', 'tensor')
All inputs are finite; a program needn't handle non-finite values.
Results may differ from a plain program's by a relative error of at most 0.023.
Values may be sent and summed in bfloat16 or wider, within the bound.
A program may use at most 128 MiB of HBM per device.

v0:
```python
import jax
import jax.numpy as jnp
from jax import lax
from jax.sharding import PartitionSpec as P

QBLOCK = 512


EPS = 1e-06
ROPE_BASE = 1000000.0
MASKED = -1e30


def norm_rows(values, gain):
    inverse = lax.rsqrt(jnp.mean(values * values, axis=-1, keepdims=True) + EPS)
    return (values * inverse * gain, inverse)


def norm_back(values, inverse, gain, upstream):
    entries = values.shape[-1]
    scaled = upstream * gain
    folded = jnp.sum(scaled * values, axis=-1, keepdims=True)
    grad_values = inverse * scaled - values * (inverse * inverse * inverse) * folded / entries
    grad_gain = jnp.sum((upstream * values * inverse).reshape(-1, entries), axis=0)
    return (grad_values, grad_gain)


def rope_tables(length, head_size):
    half_size = head_size // 2
    positions = jnp.arange(length, dtype=jnp.float32)[:, None]
    frequency = ROPE_BASE ** (-2.0 * jnp.arange(half_size, dtype=jnp.float32) / head_size)
    rotary_angles = positions * frequency[None, :]
    return (jnp.cos(rotary_angles), jnp.sin(rotary_angles))


def rotate(values, cosine, sine):
    half_size = values.shape[-1] // 2
    first_half = values[..., :half_size]
    second_half = values[..., half_size:]
    cos_wide = cosine[:, None, :]
    sin_wide = sine[:, None, :]
    return jnp.concatenate(
        [
            first_half * cos_wide - second_half * sin_wide,
            second_half * cos_wide + first_half * sin_wide,
        ],
        axis=-1,
    )


def unrotate(grads, cosine, sine):
    half_size = grads.shape[-1] // 2
    first_half = grads[..., :half_size]
    second_half = grads[..., half_size:]
    cos_wide = cosine[:, None, :]
    sin_wide = sine[:, None, :]
    return jnp.concatenate(
        [
            first_half * cos_wide + second_half * sin_wide,
            second_half * cos_wide - first_half * sin_wide,
        ],
        axis=-1,
    )


def contract_rows(left, right):
    return lax.dot_general(
        left, right, (((0,), (0,)), ((), ())), preferred_element_type=jnp.float32
    )


def times_transposed(left, right):
    return lax.dot_general(
        left, right, (((1,), (1,)), ((), ())), preferred_element_type=jnp.float32
    )


def local(
    tokens,
    cotangent,
    attn_gain,
    mlp_gain,
    query_gain,
    key_gain,
    w_query,
    key_weight,
    value_weight,
    w_out,
    w_gate,
    w_up,
    w_down,
):
    query_full, key_full, value_full, out_full, gate_full, up_full, down_full = (
        lax.all_gather(w_query, "dp", axis=0, tiled=True),
        lax.all_gather(key_weight, "dp", axis=0, tiled=True),
        lax.all_gather(value_weight, "dp", axis=0, tiled=True),
        lax.all_gather(w_out, "dp", axis=0, tiled=True),
        lax.all_gather(w_gate, "dp", axis=0, tiled=True),
        lax.all_gather(w_up, "dp", axis=0, tiled=True),
        lax.all_gather(w_down, "dp", axis=0, tiled=True),
    )
    head_size = query_gain.shape[0]
    heads_q = w_query.shape[1] // head_size
    heads_kv = key_weight.shape[1] // head_size
    group_size = heads_q // heads_kv
    rows_f = tokens.astype(jnp.float32)
    normed, inverse_one = norm_rows(rows_f, attn_gain)
    normed_all = lax.all_gather(normed.astype(jnp.bfloat16), "tensor", axis=0, tiled=True)
    length = normed_all.shape[0]
    q_lin = jnp.dot(normed_all, query_full, preferred_element_type=jnp.float32).reshape(
        length, heads_q, head_size
    )
    k_lin = jnp.dot(normed_all, key_full, preferred_element_type=jnp.float32).reshape(
        length, heads_kv, head_size
    )
    v_low = (
        jnp.dot(normed_all, value_full, preferred_element_type=jnp.float32)
        .astype(jnp.bfloat16)
        .reshape(length, heads_kv, head_size)
    )
    cosine, sine = rope_tables(length, head_size)
    q_normed, q_inverse = norm_rows(q_lin, query_gain)
    k_normed, k_inverse = norm_rows(k_lin, key_gain)
    q_rot = rotate(q_normed, cosine, sine).astype(jnp.bfloat16)
    k_rot = rotate(k_normed, cosine, sine).astype(jnp.bfloat16)
    block_rows = min(QBLOCK, length)
    block_count = length // block_rows
    q_blocks = q_rot.reshape(block_count, block_rows, heads_kv, group_size, head_size)
    block_ids = jnp.arange(block_count, dtype=jnp.int32)
    score_scale = head_size ** (-0.5)
    col_pos = jnp.arange(length, dtype=jnp.int32)

    def block_scores(query_block, block_id):
        scores = (
            jnp.einsum("bkgd,lkd->kgbl", query_block, k_rot, preferred_element_type=jnp.float32)
            * score_scale
        )
        row_pos = block_id * block_rows + jnp.arange(block_rows, dtype=jnp.int32)
        causal_keep = col_pos[None, :] <= row_pos[:, None]
        return jnp.where(causal_keep, scores, MASKED)

    def forward_block(block_pair):
        scores = block_scores(block_pair[0], block_pair[1])
        row_peak = jnp.max(scores, axis=-1, keepdims=True)
        raised = jnp.exp(scores - row_peak)
        row_total = jnp.sum(raised, axis=-1, keepdims=True)
        weights_low = (raised / row_total).astype(jnp.bfloat16)
        attended = jnp.einsum(
            "kgbl,lkd->bkgd", weights_low, v_low, preferred_element_type=jnp.float32
        )
        return (attended.astype(jnp.bfloat16), row_peak + jnp.log(row_total))

    attended_blocks, log_totals = lax.map(forward_block, (q_blocks, block_ids))
    attended = attended_blocks.reshape(length, heads_q * head_size)
    middle = rows_f + lax.psum_scatter(
        times_transposed(attended, out_full), "tensor", scatter_dimension=0, tiled=True
    )
    normed_mlp, inverse_two = norm_rows(middle, mlp_gain)
    normed_mlp_all = lax.all_gather(normed_mlp.astype(jnp.bfloat16), "tensor", axis=0, tiled=True)
    gate_lin = jnp.dot(normed_mlp_all, gate_full, preferred_element_type=jnp.float32)
    up_lin = jnp.dot(normed_mlp_all, up_full, preferred_element_type=jnp.float32)
    sigmoid_gate = jax.nn.sigmoid(gate_lin)
    activated = gate_lin * sigmoid_gate
    hidden = (activated * up_lin).astype(jnp.bfloat16)
    result = (
        middle
        + lax.psum_scatter(
            times_transposed(hidden, down_full).astype(jnp.bfloat16),
            "tensor",
            scatter_dimension=0,
            tiled=True,
        ).astype(jnp.float32)
    ).astype(jnp.bfloat16)
    cot_all = lax.all_gather(cotangent, "tensor", axis=0, tiled=True)
    d_hidden = jnp.dot(cot_all, down_full, preferred_element_type=jnp.float32)
    down_part = contract_rows(cot_all, hidden)
    d_gate = (d_hidden * up_lin * sigmoid_gate * (1.0 + gate_lin * (1.0 - sigmoid_gate))).astype(
        jnp.bfloat16
    )
    d_up = (d_hidden * activated).astype(jnp.bfloat16)
    gate_part = contract_rows(normed_mlp_all, d_gate)
    up_part = contract_rows(normed_mlp_all, d_up)
    d_normed_mlp = lax.psum_scatter(
        (times_transposed(d_gate, gate_full) + times_transposed(d_up, up_full)).astype(
            jnp.bfloat16
        ),
        "tensor",
        scatter_dimension=0,
        tiled=True,
    ).astype(jnp.float32)
    d_middle_norm, mlp_gain_part = norm_back(middle, inverse_two, mlp_gain, d_normed_mlp)
    d_middle = cotangent.astype(jnp.float32) + d_middle_norm
    d_attn_all = lax.all_gather(d_middle.astype(jnp.bfloat16), "tensor", axis=0, tiled=True)
    out_part = contract_rows(d_attn_all, attended)
    d_attended = jnp.dot(d_attn_all, out_full, preferred_element_type=jnp.float32).astype(
        jnp.bfloat16
    )
    d_blocks = d_attended.reshape(block_count, block_rows, heads_kv, group_size, head_size)

    def backward_block(carry_pair, block_items):
        key_acc, value_acc = carry_pair
        query_block, grad_block, log_total, block_id = block_items
        scores = block_scores(query_block, block_id)
        weights = jnp.exp(scores - log_total)
        weights_low = weights.astype(jnp.bfloat16)
        value_acc = value_acc + jnp.einsum(
            "kgbl,bkgd->lkd", weights_low, grad_block, preferred_element_type=jnp.float32
        )
        d_weights = jnp.einsum(
            "bkgd,lkd->kgbl", grad_block, v_low, preferred_element_type=jnp.float32
        )
        row_delta = jnp.sum(d_weights * weights, axis=-1, keepdims=True)
        d_scores = (weights * (d_weights - row_delta)).astype(jnp.bfloat16)
        d_query = (
            jnp.einsum("kgbl,lkd->bkgd", d_scores, k_rot, preferred_element_type=jnp.float32)
            * score_scale
        )
        key_acc = (
            key_acc
            + jnp.einsum(
                "kgbl,bkgd->lkd", d_scores, query_block, preferred_element_type=jnp.float32
            )
            * score_scale
        )
        return ((key_acc, value_acc), d_query)

    zero_grads = jnp.zeros((length, heads_kv, head_size), jnp.float32)
    (d_key, d_value), d_query_blocks = lax.scan(
        backward_block, (zero_grads, zero_grads), (q_blocks, d_blocks, log_totals, block_ids)
    )
    d_query = d_query_blocks.reshape(length, heads_q, head_size)
    d_q_lin, query_gain_part = norm_back(
        q_lin, q_inverse, query_gain, unrotate(d_query, cosine, sine)
    )
    d_k_lin, key_gain_part = norm_back(k_lin, k_inverse, key_gain, unrotate(d_key, cosine, sine))
    d_q_low = d_q_lin.reshape(length, heads_q * head_size).astype(jnp.bfloat16)
    d_k_low = d_k_lin.reshape(length, heads_kv * head_size).astype(jnp.bfloat16)
    d_v_low = d_value.reshape(length, heads_kv * head_size).astype(jnp.bfloat16)
    query_part = contract_rows(normed_all, d_q_low)
    key_part = contract_rows(normed_all, d_k_low)
    value_part = contract_rows(normed_all, d_v_low)
    d_normed = lax.psum_scatter(
        (
            times_transposed(d_q_low, query_full)
            + times_transposed(d_k_low, key_full)
            + times_transposed(d_v_low, value_full)
        ).astype(jnp.bfloat16),
        "tensor",
        scatter_dimension=0,
        tiled=True,
    ).astype(jnp.float32)
    d_rows_norm, attn_gain_part = norm_back(rows_f, inverse_one, attn_gain, d_normed)
    tokens_grad = d_middle + d_rows_norm
    attn_gain_grad, mlp_gain_grad, query_gain_grad, key_gain_grad = lax.psum(
        (attn_gain_part, mlp_gain_part, query_gain_part, key_gain_part), ("dp", "tensor")
    )
    query_grad, key_grad, value_grad, out_grad, gate_grad, up_grad, down_grad = (
        lax.psum_scatter(
            query_part.astype(jnp.bfloat16), "dp", scatter_dimension=0, tiled=True
        ).astype(jnp.float32),
        lax.psum_scatter(
            key_part.astype(jnp.bfloat16), "dp", scatter_dimension=0, tiled=True
        ).astype(jnp.float32),
        lax.psum_scatter(
            value_part.astype(jnp.bfloat16), "dp", scatter_dimension=0, tiled=True
        ).astype(jnp.float32),
        lax.psum_scatter(
            out_part.astype(jnp.bfloat16), "dp", scatter_dimension=0, tiled=True
        ).astype(jnp.float32),
        lax.psum_scatter(
            gate_part.astype(jnp.bfloat16), "dp", scatter_dimension=0, tiled=True
        ).astype(jnp.float32),
        lax.psum_scatter(
            up_part.astype(jnp.bfloat16), "dp", scatter_dimension=0, tiled=True
        ).astype(jnp.float32),
        lax.psum_scatter(
            down_part.astype(jnp.bfloat16), "dp", scatter_dimension=0, tiled=True
        ).astype(jnp.float32),
    )
    return (
        result,
        tokens_grad,
        attn_gain_grad,
        mlp_gain_grad,
        query_gain_grad,
        key_gain_grad,
        query_grad,
        key_grad,
        value_grad,
        out_grad,
        gate_grad,
        up_grad,
        down_grad,
    )


def solution(mesh):
    placed = (
        P(("dp", "tensor"), None),
        P(("dp", "tensor"), None),
        P(),
        P(),
        P(),
        P(),
        P("dp", "tensor"),
        P("dp", "tensor"),
        P("dp", "tensor"),
        P("dp", "tensor"),
        P("dp", "tensor"),
        P("dp", "tensor"),
        P("dp", "tensor"),
    )
    return jax.shard_map(
        local,
        mesh=mesh,
        in_specs=placed,
        out_specs=(
            P(("dp", "tensor"), None),
            P(("dp", "tensor"), None),
            P(),
            P(),
            P(),
            P(),
            P("dp", "tensor"),
            P("dp", "tensor"),
            P("dp", "tensor"),
            P("dp", "tensor"),
            P("dp", "tensor"),
            P("dp", "tensor"),
            P("dp", "tensor"),
        ),
        check_vma=False,
    )
```

profile of v0, /device:TPU:0, one launch (start us, length us, event | category | flops | bytes accessed | tf_op | source)
XLA Modules:
  0.0 1335.6 jit_solution(17244932325753228233)
XLA Ops:
  12.7 23.3 %all_gather.35 = bf16[2048,128]{1,0:T(8,128)(2,1)S(1)} all-gather(bf16[128,128]{1,0:T(8,128)(2,1)} %param.24), channel_id=1, replica_groups=mesh['dp'=16,'tensor'=8] {'dp'}, dimensions={0}, use_global_device_ids=true | all-gather | bytes 557056 | tf_op jit(solution)/shard_map/all_gather | solution.py:95
  36.0 19.8 %all_gather.36 = bf16[2048,128]{1,0:T(8,128)(2,1)} all-gather(bf16[128,128]{1,0:T(8,128)(2,1)} %param.25), channel_id=1, replica_groups=mesh['dp'=16,'tensor'=8] {'dp'}, dimensions={0}, use_global_device_ids=true | all-gather | bytes 557056 | tf_op jit(solution)/shard_map/all_gather | solution.py:96
  57.8 27.6 %all-gather.10.cloned.1.call-done = bf16[1024,2048]{1,0:T(8,128)(2,1)} async-done(((bf16[128,2048]{1,0:T(8,128)(2,1)}), bf16[1024,2048]{1,0:T(8,128)(2,1)}) %all-gather.10.cloned.1.call-update) | async-done | bytes 4194320 | tf_op jit(solution)/shard_map/all_gather | solution.py:108
  92.2 25.7 %all-gather.12.cloned.1.call-done = bf16[2048,256]{1,0:T(8,128)(2,1)} async-done(((bf16[128,256]{1,0:T(8,128)(2,1)}), bf16[2048,256]{1,0:T(8,128)(2,1)}) %all-gather.12.cloned.1.call-update) | async-done | bytes 1048592 | tf_op jit(solution)/shard_map/all_gather | solution.py:94
  131.9 13.3 while.28
  158.9 113.6 %reduce-scatter.14.cloned.1.call-done = f32[128,2048]{1,0:T(8,128)} async-done(((f32[1024,2048]{1,0:T(8,128)}), f32[128,2048]{1,0:T(8,128)}) %reduce-scatter.14.cloned.1.call-update) | async-done | bytes 1048592 | tf_op jit(solution)/shard_map/reduce_scatter | solution.py:155
  277.7 30.4 %all-gather.20.cloned.1.call-done = bf16[2048,768]{1,0:T(8,128)(2,1)} async-done(((bf16[128,768]{1,0:T(8,128)(2,1)}), bf16[2048,768]{1,0:T(8,128)(2,1)}) %all-gather.20.cloned.1.call-update) | async-done | bytes 3145744 | tf_op jit(solution)/shard_map/all_gather | solution.py:99
  308.1 74.3 %all-gather.16.cloned.1.call-done = bf16[1024,2048]{1,0:T(8,128)(2,1)} async-done(((bf16[128,2048]{1,0:T(8,128)(2,1)}), bf16[1024,2048]{1,0:T(8,128)(2,1)}) %all-gather.16.cloned.1.call-update) | async-done | bytes 4194320 | tf_op jit(solution)/shard_map/all_gather | solution.py:159
  390.7 27.5 %all-gather.18.cloned.1.call-done = bf16[2048,768]{1,0:T(8,128)(2,1)} async-done(((bf16[128,768]{1,0:T(8,128)(2,1)}), bf16[2048,768]{1,0:T(8,128)(2,1)}) %all-gather.18.cloned.1.call-update) | async-done | bytes 3145744 | tf_op jit(solution)/shard_map/all_gather | solution.py:98
  426.5 29.5 %all-gather.22.cloned.1.call-done = bf16[2048,768]{1,0:T(8,128)(2,1)} async-done(((bf16[128,768]{1,0:T(8,128)(2,1)}), bf16[2048,768]{1,0:T(8,128)(2,1)}) %all-gather.22.cloned.1.call-update) | async-done | bytes 3145744 | tf_op jit(solution)/shard_map/all_gather | solution.py:100
  456.0 73.8 %all-gather.24.cloned.1.call-done = bf16[1024,2048]{1,0:T(8,128)(2,1)} async-done(((bf16[128,2048]{1,0:T(8,128)(2,1)}), bf16[1024,2048]{1,0:T(8,128)(2,1)}) %all-gather.24.cloned.1.call-update) | async-done | bytes 4194320 | tf_op jit(solution)/shard_map/all_gather | solution.py:174
  529.9 10.6 multiply_convert_fusion
  549.3 82.5 %reduce-scatter.18.cloned.1.call-done = bf16[128,2048]{1,0:T(8,128)(2,1)} async-done(((bf16[1024,2048]{1,0:T(8,128)(2,1)}), bf16[128,2048]{1,0:T(8,128)(2,1)}) %reduce-scatter.18.cloned.1.call-update) | async-done | bytes 524304 | tf_op jit(solution)/shard_map/reduce_scatter | solution.py:183
  664.3 41.4 %all-gather.26.cloned.1.call-done = bf16[1024,2048]{1,0:T(8,128)(2,1)} async-done(((bf16[128,2048]{1,0:T(8,128)(2,1)}), bf16[1024,2048]{1,0:T(8,128)(2,1)}) %all-gather.26.cloned.1.call-update) | async-done | bytes 4194320 | tf_op jit(solution)/shard_map/all_gather | solution.py:193
  710.4 20.8 %while.29 = (s32[]{:T(128)}, f32[1024,1,128]{0,2,1:T(8,128)S(1)}, f32[1024,1,128]{0,2,1:T(8,128)}, f32[2,512,1,2,128]{4,1,0,3,2:T(8,128)}, bf16[2,512,1,2,128]{4...) while((s32[]{:T(128)}, f32[1024,1,128]{0,2,1:T(8,128)S(1)}, ...), condition=%wide.region_14.15_spmd.clone, body=%wide.region_12.14_spmd.clone.sunk | while | flops 1359216128 | bytes 51151148 | solution.py:228
  784.0 53.2 %reduce-scatter.32.cloned.1.call-done = bf16[128,768]{1,0:T(8,128)(2,1)} async-done(((bf16[2048,768]{1,0:T(8,128)(2,1)}), bf16[128,768]{1,0:T(8,128)(2,1)}) %reduce-scatter.32.cloned.1.call-update) | async-done | bytes 196624 | tf_op jit(solution)/shard_map/reduce_scatter | solution.py:273
  838.9 64.2 %reduce-scatter.30.cloned.1.call-done = bf16[128,768]{1,0:T(8,128)(2,1)} async-done(((bf16[2048,768]{1,0:T(8,128)(2,1)}), bf16[128,768]{1,0:T(8,128)(2,1)}) %reduce-scatter.30.cloned.1.call-update) | async-done | bytes 196624 | tf_op jit(solution)/shard_map/reduce_scatter | solution.py:270
  908.5 56.0 %reduce-scatter.24.cloned.1.call-done = bf16[128,128]{1,0:T(8,128)(2,1)} async-done(((bf16[2048,128]{1,0:T(8,128)(2,1)}), bf16[128,128]{1,0:T(8,128)(2,1)}) %reduce-scatter.24.cloned.1.call-update) | async-done | bytes 32784 | tf_op jit(solution)/shard_map/reduce_scatter | solution.py:261
  965.9 60.1 %reduce-scatter.26.cloned.1.call-done = bf16[128,128]{1,0:T(8,128)(2,1)} async-done(((bf16[2048,128]{1,0:T(8,128)(2,1)}), bf16[128,128]{1,0:T(8,128)(2,1)}) %reduce-scatter.26.cloned.1.call-update) | async-done | bytes 32784 | tf_op jit(solution)/shard_map/reduce_scatter | solution.py:264
  1027.4 61.0 %reduce-scatter.28.cloned.1.call-done = bf16[128,256]{1,0:T(8,128)(2,1)} async-done(((bf16[2048,256]{1,0:T(8,128)(2,1)}), bf16[128,256]{1,0:T(8,128)(2,1)}) %reduce-scatter.28.cloned.1.call-update) | async-done | bytes 65552 | tf_op jit(solution)/shard_map/reduce_scatter | solution.py:267
  1089.9 60.9 %reduce-scatter.22.cloned.1.call-done = bf16[128,256]{1,0:T(8,128)(2,1)} async-done(((bf16[2048,256]{1,0:T(8,128)(2,1)}), bf16[128,256]{1,0:T(8,128)(2,1)}) %reduce-scatter.22.cloned.1.call-update) | async-done | bytes 65552 | tf_op jit(solution)/shard_map/reduce_scatter | solution.py:258
  1152.4 85.2 %reduce-scatter.20.cloned.1.call-done = bf16[128,2048]{1,0:T(8,128)(2,1)} async-done(((bf16[1024,2048]{1,0:T(8,128)(2,1)}), bf16[128,2048]{1,0:T(8,128)(2,1)}) %reduce-scatter.20.cloned.1.call-update) | async-done | bytes 524304 | tf_op jit(solution)/shard_map/reduce_scatter | solution.py:242
  1238.9 70.8 %all-reduce = (f32[2048]{0:T(1024)}, f32[2048]{0:T(1024)}, f32[128]{0:T(128)}, f32[128]{0:T(128)}) all-reduce(f32[2048]{0:T(1024)S(1)} %get-tuple-element.265, f32[2048]{0:T(1024)S(1)} %get-tuple-element.261, f32[128]{0:T(128)S(1)} %fusion.79, f32[128]{0:T(128)S(1)} %get-tuple-element.263), channel_id=1, replica_groups=mesh['dp'=16,'tensor'=8] {'dp','tensor'}, use_global_device_ids=true, to_apply=%region_20.21 | all-reduce | flops 4352 | bytes 34816 | tf_op jit(solution)/shard_map/psum | solution.py:254
  1309.7 15.7 %reduce-scatter.16.cloned.1.call-done = bf16[128,2048]{1,0:T(8,128)(2,1)} async-done(((bf16[1024,2048]{1,0:T(8,128)(2,1)}), bf16[128,2048]{1,0:T(8,128)(2,1)}) %reduce-scatter.16.cloned.1.call-update) | async-done | bytes 524304 | tf_op jit(solution)/shard_map/reduce_scatter | solution.py:167
  (269 shorter events, 210.2 us)
Async XLA Ops:
  7.2 78.2 %all-gather.10.cloned.1.call-start = ((), (), s32[]{:S(2)}) async-start(), calls=%async_computation.11 | async-start | bytes 4718592 | tf_op jit(solution)/shard_map/all_gather | solution.py:108
  11.1 106.8 %all-gather.12.cloned.1.call-start = ((), (), s32[]{:S(2)}) async-start(), calls=%async_computation.12 | async-start | bytes 1114112 | tf_op jit(solution)/shard_map/all_gather | solution.py:94
  11.9 140.4 %all-gather.14.cloned.1.call-start = ((), (), s32[]{:S(2)}) async-start(), calls=%async_computation.13 | async-start | bytes 1114112 | tf_op jit(solution)/shard_map/all_gather | solution.py:97
  12.6 259.9 %reduce-scatter.14.cloned.1.call-start = ((), (), s32[]{:S(2)}) async-start(), calls=%async_computation.14 | async-start | bytes 9437184 | tf_op jit(solution)/shard_map/reduce_scatter | solution.py:155
  158.2 149.9 %all-gather.20.cloned.1.call-start = ((), (), s32[]{:S(2)}) async-start(), calls=%async_computation.17 | async-start | bytes 3342336 | tf_op jit(solution)/shard_map/all_gather | solution.py:99
  158.8 223.6 %all-gather.16.cloned.1.call-start = ((), (), s32[]{:S(2)}) async-start(), calls=%async_computation.15 | async-start | bytes 4718592 | tf_op jit(solution)/shard_map/all_gather | solution.py:159
  274.9 143.3 %all-gather.18.cloned.1.call-start = ((), (), s32[]{:S(2)}) async-start(), calls=%async_computation.16 | async-start | bytes 3342336 | tf_op jit(solution)/shard_map/all_gather | solution.py:98
  275.7 180.4 %all-gather.22.cloned.1.call-start = ((), (), s32[]{:S(2)}) async-start(), calls=%async_computation.18 | async-start | bytes 3342336 | tf_op jit(solution)/shard_map/all_gather | solution.py:100
  276.4 253.5 %all-gather.24.cloned.1.call-start = ((), (), s32[]{:S(2)}) async-start(), calls=%async_computation.20 | async-start | bytes 4718592 | tf_op jit(solution)/shard_map/all_gather | solution.py:174
  277.1 354.7 %reduce-scatter.18.cloned.1.call-start = ((), (), s32[]{:S(2)}) async-start(), calls=%async_computation.21 | async-start | bytes 4718592 | tf_op jit(solution)/shard_map/reduce_scatter | solution.py:183
  549.2 156.5 %all-gather.26.cloned.1.call-start = ((), (), s32[]{:S(2)}) async-start(), calls=%async_computation.22 | async-start | bytes 4718592 | tf_op jit(solution)/shard_map/all_gather | solution.py:193
  635.5 146.5 %reduce-scatter.34.cloned.1.call-start = ((), (), s32[]{:S(2)}) async-start(), calls=%async_computation.30 | async-start | bytes 3342336
  648.1 189.2 %reduce-scatter.32.cloned.1.call-start = ((), (), s32[]{:S(2)}) async-start(), calls=%async_computation.29 | async-start | bytes 3342336 | tf_op jit(solution)/shard_map/reduce_scatter | solution.py:273
  656.0 247.1 %reduce-scatter.30.cloned.1.call-start = ((), (), s32[]{:S(2)}) async-start(), calls=%async_computation.28 | async-start | bytes 3342336 | tf_op jit(solution)/shard_map/reduce_scatter | solution.py:270
  664.1 300.4 %reduce-scatter.24.cloned.1.call-start = ((), (), s32[]{:S(2)}) async-start(), calls=%async_computation.25 | async-start | bytes 557056 | tf_op jit(solution)/shard_map/reduce_scatter | solution.py:261
  737.1 288.9 %reduce-scatter.26.cloned.1.call-start = ((), (), s32[]{:S(2)}) async-start(), calls=%async_computation.26 | async-start | bytes 557056 | tf_op jit(solution)/shard_map/reduce_scatter | solution.py:264
  741.6 346.8 %reduce-scatter.28.cloned.1.call-start = ((), (), s32[]{:S(2)}) async-start(), calls=%async_computation.27 | async-start | bytes 1114112 | tf_op jit(solution)/shard_map/reduce_scatter | solution.py:267
  746.4 404.5 %reduce-scatter.22.cloned.1.call-start = ((), (), s32[]{:S(2)}) async-start(), calls=%async_computation.24 | async-start | bytes 1114112 | tf_op jit(solution)/shard_map/reduce_scatter | solution.py:258
  762.3 475.2 %reduce-scatter.20.cloned.1.call-start = ((), (), s32[]{:S(2)}) async-start(), calls=%async_computation.23 | async-start | bytes 4718592 | tf_op jit(solution)/shard_map/reduce_scatter | solution.py:242
  768.5 556.9 %reduce-scatter.16.cloned.1.call-start = ((), (), s32[]{:S(2)}) async-start(), calls=%async_computation.19 | async-start | bytes 4718592 | tf_op jit(solution)/shard_map/reduce_scatter | solution.py:167
  838.9 398.6 %copy-start.32 = (f32[2048]{0:T(1024)S(1)}, f32[2048]{0:T(1024)}, u32[]{:S(2)}) copy-start(f32[2048]{0:T(1024)} %param.19) | copy-start | bytes 24580
  838.9 398.6 %copy-start.42 = (f32[128]{0:T(128)S(1)}, f32[128]{0:T(128)}, u32[]{:S(2)}) copy-start(f32[128]{0:T(128)} %copy-done.41) | copy-start | bytes 1540
  904.9 420.5 %copy-start.14 = (bf16[128,2048]{1,0:T(8,128)(2,1)S(1)}, bf16[128,2048]{1,0:T(8,128)(2,1)}, u32[]{:S(2)}) copy-start(bf16[128,2048]{1,0:T(8,128)(2,1)} %param.18) | copy-start | bytes 1572868
  904.9 420.5 %copy-start.45 = (f32[128]{0:T(128)S(1)}, f32[128]{0:T(128)}, u32[]{:S(2)}) copy-start(f32[128]{0:T(128)} %get-tuple-element.330) | copy-start | bytes 1540
  (52 other events, 1354.8 us)
Sparse Core Ops, SparseCore 0:
  11.2 74.1 all-gather.9
  87.1 30.8 all-gather.11
  119.7 32.5 all-gather.13
  158.4 114.0 reduce-scatter.13
  274.1 33.9 all-gather.19
  311.2 71.1 all-gather.15
  384.2 33.9 all-gather.17
  420.0 35.9 all-gather.21
  458.6 71.1 all-gather.23
  549.4 82.3 reduce-scatter.17
  635.6 70.0 all-gather.25
  708.0 63.1 reduce-scatter.33
  773.6 63.6 reduce-scatter.31
  839.5 63.6 reduce-scatter.29
  905.3 59.1 reduce-scatter.23
  966.8 59.1 reduce-scatter.25
  1028.3 60.1 reduce-scatter.27
  1090.7 60.0 reduce-scatter.21
  1154.7 82.7 reduce-scatter.19
  1241.7 83.7 reduce-scatter.15
where the time goes:
time: 1340 us
  waiting for transfers between devices  994 us (74%)
  matrix products  128 us (10%)
  blocking collectives  114 us (9%)
  other arithmetic  46.2 us (3%)
  local copies, waits for them, and re-layouts  33.3 us (2%)
  between operations  15.1 us (1%)
    reduce_scatter x1, waiting for transfers between devices, local(): lax.psum_scatter(times_transposed(attended, out_full), 'tensor', scatter_...  114 us
    reduce_scatter x1, waiting for transfers between devices, local(): lax.psum_scatter((times_transposed(d_q_low, query_full) + times_transpose...  85.2 us
    reduce_scatter x1, waiting for transfers between devices, local(): lax.psum_scatter((times_transposed(d_gate, gate_full) + times_transposed(...  82.5 us
    all_gather x1, waiting for transfers between devices, local(): lax.all_gather(normed_mlp.astype(jnp.bfloat16), 'tensor', axis=0, tiled=T...  74.3 us
    all_gather x1, waiting for transfers between devices, local(): cot_all = lax.all_gather(cotangent, 'tensor', axis=0, tiled=True)  73.8 us
    psum x1, blocking collectives, local(): lax.psum((attn_gain_part, mlp_gain_part, query_gain_part, key_gain_part),...  70.8 us
    reduce_scatter x1, waiting for transfers between devices, local(): lax.psum_scatter(gate_part.astype(jnp.bfloat16), 'dp', scatter_dimension=...  64.2 us
    reduce_scatter x1, waiting for transfers between devices, local(): lax.psum_scatter(out_part.astype(jnp.bfloat16), 'dp', scatter_dimension=0...  61 us
  transfers between devices with their start and end apart: 20, of which 19 were waited for; matrix products, arithmetic and copies ran while one was open for 12% of the time, Pallas kernels for 0%

commit v1 on v0

v1 whole, which is shorter than its diff:
```python
import functools

import numpy as np
import jax
import jax.numpy as jnp
from jax import lax
from jax.experimental import pallas as pl
from jax.experimental.pallas import tpu as pltpu
from jax.sharding import PartitionSpec as P

EPS = 1e-06
ROPE_BASE = 1000000.0
MESH = pl.DeviceIdType.MESH
BF = jnp.bfloat16
F32 = jnp.float32
HEAD = 128
WIDTH = 2048
BLOCK = 128
ROWS = 1024
A_COLS = 768
B_COLS = 2304
A_CUT = 384
B_CUT = 1152
SCORE = HEAD ** -0.5
SCORE2 = HEAD ** -0.5 * 1.4426950408889634
VMEM_BYTES = 63 * 2**20


class Place:
    def __init__(self):
        dp = lax.axis_index("dp")
        tensor = lax.axis_index("tensor")
        self.dp = dp
        self.xlo = lax.div(dp, 8)
        self.z = lax.rem(lax.div(dp, 2), 4)
        self.c = lax.rem(dp, 2)
        self.y = lax.div(tensor, 2)
        self.xhi = lax.rem(tensor, 2)
        self.x = self.xhi * 2 + self.xlo

    def at(self, x=None, y=None, z=None, c=None):
        x = self.x if x is None else x
        y = self.y if y is None else y
        z = self.z if z is None else z
        c = self.c if c is None else c
        return (lax.rem(x, 2) * 8 + z * 2 + c, y * 2 + lax.div(x, 2))

    def sibling(self):
        return self.at(c=1 - self.c)


def ring(v, k):
    return lax.rem(v + k, 4)


def remote(src, dst, send_sem, recv_sem, target):
    return pltpu.make_async_remote_copy(
        src_ref=src, dst_ref=dst, send_sem=send_sem, recv_sem=recv_sem,
        device_id=target, device_id_type=MESH,
    )


def settle(ref, sem):
    pltpu.make_async_copy(ref, ref, sem).wait()


def rows_at(start, size):
    return pl.ds(pl.multiple_of(start, 128), size)


def greet(me, both_cores=False):
    barrier = pltpu.get_barrier_semaphore()
    others = [me.sibling()]
    for k in (1, 2, 3):
        others.append(me.at(y=ring(me.y, k)))
        if both_cores:
            others.append(me.at(y=ring(me.y, k), c=1 - me.c))
        for c in (0, 1):
            others.append(me.at(x=ring(me.x, k), c=c))
            others.append(me.at(z=ring(me.z, k), c=c))
    for other in others:
        pl.semaphore_signal(barrier, inc=1, device_id=other, device_id_type=MESH)
    return barrier, len(others)


class GatherRows:
    sems = 14

    def __init__(self, me, buf, send, recv):
        self.me, self.buf, self.send, self.recv = me, buf, send, recv

    def slot(self, c, y):
        return self.buf.at[rows_at((c * 4 + y) * BLOCK, BLOCK)]

    def to_sibling(self, y, k):
        me = self.me
        ref = self.slot(me.c, y)
        remote(ref, ref, self.send.at[4 + k], self.recv.at[4 + k], me.sibling()).start()

    def start(self):
        me = self.me
        own = self.slot(me.c, me.y)
        for k in (1, 3, 2):
            remote(own, own, self.send.at[k], self.recv.at[k], me.at(y=ring(me.y, k))).start()
        self.to_sibling(me.y, 0)

    def relay(self):
        me = self.me
        for k in (1, 3, 2):
            source = ring(me.y, 4 - k)
            settle(self.slot(me.c, source), self.recv.at[k])
            self.to_sibling(source, k)

    def finish(self):
        me = self.me
        own = self.slot(me.c, me.y)
        for k in (1, 2, 3):
            settle(own, self.send.at[k])
        for k in range(4):
            settle(own, self.send.at[4 + k])
            settle(self.slot(1 - me.c, ring(me.y, 4 - k)), self.recv.at[4 + k])


class ReduceRows:
    def __init__(self, me, sib_out, held, arrive, send, recv):
        self.me = me
        self.sib_out, self.held, self.arrive = sib_out, held, arrive
        self.send, self.recv = send, recv
        first = 1 - lax.div(me.y, 2)
        self.halves = (first, 1 - first)

    def other(self, tile):
        me = self.me
        for p, half in enumerate(self.halves):
            rows = rows_at(half * 256, 256)

            def step(j, _):
                cols = rows_at(j * 512, 512)
                self.sib_out[rows, cols] = tile((1 - me.c) * 512 + half * 256, j).astype(BF)
                return 0

            lax.fori_loop(0, 4, step, 0, unroll=True)
            remote(self.sib_out.at[rows], self.held.at[rows], self.send.at[4 + p], self.recv.at[4 + p],
                   me.sibling()).start()

    def mine(self, tile):
        me = self.me
        for p, half in enumerate(self.halves):
            rows = rows_at(half * 256, 256)
            settle(self.held.at[rows], self.recv.at[4 + p])

            def step(j, _):
                cols = rows_at(j * 512, 512)
                total = tile(me.c * 512 + half * 256, j) + self.held[rows, cols].astype(F32)
                self.held[rows, cols] = total.astype(BF)
                return 0

            lax.fori_loop(0, 4, step, 0, unroll=True)
            for q in (0, 1):
                block = half * 2 + q
                k = ring(block + 4 - me.y, 0)

                def go(block=block, k=k):
                    remote(self.held.at[rows_at(block * BLOCK, BLOCK)], self.arrive.at[k - 1], self.send.at[k],
                           self.recv.at[k], me.at(y=block)).start()

                if p == 0:
                    go()
                else:
                    pl.when(block != me.y)(go)

    def wait(self):
        for k in (1, 2, 3):
            settle(self.arrive.at[k - 1], self.recv.at[k])

    def total(self, r):
        total = self.held[pl.ds(pl.multiple_of(self.me.y * BLOCK + r, 16), 16), :].astype(F32)
        for k in (1, 2, 3):
            total = total + self.arrive[k - 1, pl.ds(pl.multiple_of(r, 16), 16), :].astype(F32)
        return total

    def finish(self):
        for k in (1, 2, 3):
            settle(self.arrive.at[k - 1], self.send.at[k])
        for p in (0, 1):
            settle(self.sib_out.at[rows_at(0, 256)], self.send.at[4 + p])


class GatherWeights:
    def __init__(self, me, shard, full, cut, send, recv):
        self.me, self.shard, self.full = me, shard, full
        self.cols = (pl.ds(0, cut), pl.ds(cut, shard.shape[1] - cut))
        self.send, self.recv = send, recv

    def slot(self, way, dp):
        return self.full.at[rows_at(dp * BLOCK, BLOCK), self.cols[way]]

    def first(self):
        me = self.me
        home = me.xhi
        for way in (0, 1):
            src = self.shard.at[:, self.cols[way]]
            dst = self.slot(way, me.dp)
            inbox = self.recv.at[(me.xlo * 2 + me.c) if way == 0 else (10 + me.z * 2 + me.c)]
            base = 0 if way == 0 else 10
            for k in (1, 3, 2):
                target = me.at(x=ring(me.x, k), c=home) if way == 0 else me.at(z=ring(me.z, k), c=home)
                remote(src, dst, self.send.at[base + k], inbox, target).start()

            @pl.when(me.c == home)
            def _():
                pltpu.make_async_copy(src, dst, inbox).start()

            @pl.when(me.c != home)
            def _():
                remote(src, dst, self.send.at[base], inbox, me.sibling()).start()

    def second(self):
        me = self.me
        for xlo in (0, 1):
            for c in (0, 1):
                settle(self.slot(0, xlo * 8 + me.z * 2 + c), self.recv.at[xlo * 2 + c])
        for k in (1, 3, 2):
            for xlo in (0, 1):
                ref = self.pair(xlo, me.z)
                i = 4 + xlo * 3 + k - 1
                remote(ref, ref, self.send.at[i], self.recv.at[i], me.at(z=ring(me.z, k))).start()

        @pl.when(me.c == me.xhi)
        def _():
            for z in range(4):
                for c in (0, 1):
                    settle(self.slot(1, me.xlo * 8 + z * 2 + c), self.recv.at[10 + z * 2 + c])
            ref = self.half(me.xlo)
            for k in (1, 3, 2):
                remote(ref, ref, self.send.at[18 + k], self.recv.at[18 + me.xlo], me.at(x=ring(me.x, k))).start()

    def pair(self, xlo, z):
        return self.full.at[rows_at(xlo * 1024 + z * 256, 256), self.cols[0]]

    def half(self, xlo):
        return self.full.at[rows_at(xlo * 1024, 1024), self.cols[1]]

    def arrived(self):
        me = self.me
        for k in (1, 2, 3):
            for xlo in (0, 1):
                settle(self.pair(xlo, ring(me.z, 4 - k)), self.recv.at[4 + xlo * 3 + k - 1])
        for xlo in (0, 1):
            @pl.when(jnp.logical_or(me.c != me.xhi, me.xlo != xlo))
            def _():
                settle(self.half(xlo), self.recv.at[18 + xlo])

    def finish(self):
        me = self.me
        for way in (0, 1):
            src = self.shard.at[:, self.cols[way]]
            base = 0 if way == 0 else 10
            for k in (1, 2, 3):
                settle(src, self.send.at[base + k])

            @pl.when(me.c != me.xhi)
            def _():
                settle(src, self.send.at[base])
        for k in (1, 2, 3):
            for xlo in (0, 1):
                settle(self.pair(xlo, me.z), self.send.at[4 + xlo * 3 + k - 1])

        @pl.when(me.c == me.xhi)
        def _():
            for k in (1, 2, 3):
                settle(self.half(me.xlo), self.send.at[18 + k])


def dot(left, right):
    return jnp.dot(left, right, preferred_element_type=F32)


def dot_t(left, right):
    return lax.dot_general(left, right, (((1,), (1,)), ((), ())), preferred_element_type=F32)


def inverse_of(values):
    return lax.rsqrt(jnp.mean(values * values, axis=-1, keepdims=True) + EPS)


def turn(values, cosine, sine):
    return values * cosine + pltpu.roll(values, 64, 1) * sine


def forward_kernel(
    tokens, cot, attn_gain, mlp_gain, query_gain, key_gain, wq, wk, wv, wo, wg, wu, wd, cosine, sine,
    n_out, cot_out, n2_out, a_out, b_out, qlin_out, klin_out, qrot_out, kv_out, o_out, mid_out,
    n, cota, n2, a, b, a_shard, b_shard, qlin, klin, qrot, kv, o, mid, sib_out, held, arrive,
    n_send, n_recv, c_send, c_recv, n2_send, n2_recv, a_send, a_recv, b_send, b_recv, r_send, r_recv,
    kv_sem, out_sem,
):
    me = Place()
    barrier, count = greet(me)
    a_shard[:, 0:256] = wq[...]
    a_shard[:, 256:384] = wk[...]
    a_shard[:, 384:512] = wv[...]
    a_shard[:, 512:768] = wo[...]
    b_shard[:, 0:768] = wg[...]
    b_shard[:, 768:1536] = wu[...]
    b_shard[:, 1536:2304] = wd[...]
    own = (me.c * 4 + me.y) * BLOCK

    def norm_one(i, _):
        rows = pl.ds(pl.multiple_of(i * 16, 16), 16)
        x = tokens[rows, :].astype(F32)
        n[pl.ds(pl.multiple_of(own + i * 16, 16), 16), :] = (x * inverse_of(x) * attn_gain[...]).astype(BF)
        return 0

    lax.fori_loop(0, 8, norm_one, 0)
    cota[rows_at(own, BLOCK), :] = cot[...]
    pl.semaphore_wait(barrier, count)

    weights_a = GatherWeights(me, a_shard, a, A_CUT, a_send, a_recv)
    weights_b = GatherWeights(me, b_shard, b, B_CUT, b_send, b_recv)
    rows_n = GatherRows(me, n, n_send, n_recv)
    rows_c = GatherRows(me, cota, c_send, c_recv)
    rows_n2 = GatherRows(me, n2, n2_send, n2_recv)
    weights_a.first()
    rows_n.start()
    weights_a.second()
    weights_b.first()
    rows_n.relay()
    rows_n.finish()
    rows_c.start()
    weights_a.arrived()
    outs = []

    def out(src, dst):
        copy = pltpu.make_async_copy(src, dst, out_sem.at[len(outs)])
        copy.start()
        outs.append(copy)

    out(n, n_out)
    out(a, a_out)

    def project(s, _):
        rows = rows_at(s * 512, 512)
        x = n[rows, :]
        cos, sin = cosine[me.xhi], sine[me.xhi]
        q = dot(x, a[:, 0:256])
        qlin[rows, :] = q
        for g in (0, 1):
            u = q[:, g * 128:(g + 1) * 128]
            u = turn(u * inverse_of(u) * query_gain[...], cos, sin).astype(BF)
            for block in range(4):
                qrot[rows_at(s * 1024 + block * 256 + g * 128, 128), :] = u[block * 128:(block + 1) * 128]
        k = dot(x, a[:, 256:512])
        klin[rows, :] = k[:, 0:128]
        u = k[:, 0:128]
        kv[0, rows, :] = turn(u * inverse_of(u) * key_gain[...], cos, sin).astype(BF)
        kv[1, rows, :] = k[:, 128:256].astype(BF)
        return 0

    lax.fori_loop(0, 2, project, 0)
    swap = remote(kv.at[0:2], kv.at[2:4], kv_sem.at[0], kv_sem.at[1], me.at(x=ring(me.x, 2)))
    swap.start()
    out(qlin, qlin_out)
    out(klin, klin_out)
    out(qrot, qrot_out)
    weights_b.second()
    swap.wait()
    out(kv, kv_out)

    def attend(s, _):
        for block in range(4):
            keys = rows_at(s * 512, (block + 1) * 128)
            q = qrot[rows_at(s * 1024 + block * 256, 256), :]
            shape = (256, (block + 1) * 128)
            row = lax.rem(lax.broadcasted_iota(jnp.int32, shape, 0), 128)
            col = lax.broadcasted_iota(jnp.int32, shape, 1)
            near = jnp.where(col <= row + block * 128, jnp.exp2(dot_t(q, kv[0, keys, :]) * SCORE2), 0.0)
            far = jnp.where(col < (block + me.xhi) * 128, jnp.exp2(dot_t(q, kv[2, keys, :]) * SCORE2), 0.0)
            total = jnp.sum(near, axis=-1, keepdims=True) + jnp.sum(far, axis=-1, keepdims=True)
            got = dot(near.astype(BF), kv[1, keys, :]) + dot(far.astype(BF), kv[3, keys, :])
            got = (got / total).astype(BF)
            rows = rows_at(s * 512 + block * 128, 128)
            o[rows, 0:128] = got[0:128]
            o[rows, 128:256] = got[128:256]
        return 0

    lax.fori_loop(0, 2, attend, 0)
    rows_c.relay()
    out(o, o_out)
    sums = ReduceRows(me, sib_out, held, arrive, r_send, r_recv)

    def branch(row, j):
        return dot_t(o[rows_at(row, 256), :], a[rows_at(j * 512, 512), 512:768])

    sums.other(branch)
    sums.mine(branch)
    rows_c.finish()
    out(cota, cot_out)
    sums.wait()

    def norm_two(i, _):
        rows = pl.ds(pl.multiple_of(i * 16, 16), 16)
        x = tokens[rows, :].astype(F32) + sums.total(i * 16)
        mid[rows, :] = x
        n2[pl.ds(pl.multiple_of(own + i * 16, 16), 16), :] = (x * inverse_of(x) * mlp_gain[...]).astype(BF)
        return 0

    lax.fori_loop(0, 8, norm_two, 0)
    rows_n2.start()
    out(mid, mid_out)
    weights_b.arrived()
    out(b, b_out)
    rows_n2.relay()
    rows_n2.finish()
    out(n2, n2_out)
    sums.finish()
    weights_a.finish()
    weights_b.finish()
    for copy in outs:
        copy.wait()


def forward(*args):
    shapes = [
        ((ROWS, WIDTH), BF), ((ROWS, WIDTH), BF), ((ROWS, WIDTH), BF), ((WIDTH, A_COLS), BF), ((WIDTH, B_COLS), BF),
        ((ROWS, 256), F32), ((ROWS, 128), F32), ((2 * ROWS, 128), BF), ((4, ROWS, 128), BF), ((ROWS, 256), BF),
        ((BLOCK, WIDTH), F32),
    ]
    scratch = [pltpu.VMEM(s, d) for s, d in shapes[:5]]
    scratch += [pltpu.VMEM((BLOCK, A_COLS), BF), pltpu.VMEM((BLOCK, B_COLS), BF)]
    scratch += [pltpu.VMEM(s, d) for s, d in shapes[5:]]
    scratch += [pltpu.VMEM((512, WIDTH), BF)] * 2 + [pltpu.VMEM((3, BLOCK, WIDTH), BF)]
    dma = pltpu.SemaphoreType.DMA
    scratch += [dma((8,))] * 6 + [dma((22,))] * 4 + [dma((6,))] * 2 + [dma((2,)), dma((len(shapes),))]
    return pl.pallas_call(
        forward_kernel,
        out_shape=[jax.ShapeDtypeStruct(s, d) for s, d in shapes],
        in_specs=[pl.BlockSpec(memory_space=pltpu.VMEM)] * len(args),
        out_specs=[pl.BlockSpec(memory_space=pl.ANY)] * len(shapes),
        scratch_shapes=scratch,
        compiler_params=pltpu.CompilerParams(
            collective_id=1, has_side_effects=True, vmem_limit_bytes=VMEM_BYTES),
        name="forward_part",
    )(*args)


def rope_tables():
    frequency = ROPE_BASE ** (-2.0 * np.arange(64, dtype=np.float64) / HEAD)
    angle = np.arange(1024, dtype=np.float64)[:, None] * frequency[None, :]
    cos = np.concatenate([np.cos(angle), np.cos(angle)], axis=1).astype(np.float32)
    sin = np.concatenate([-np.sin(angle), np.sin(angle)], axis=1).astype(np.float32)
    pick = lambda t: t.reshape(4, 2, 128, 128).transpose(1, 0, 2, 3).reshape(2, 512, 128)
    return pick(cos), pick(sin)


class ReduceWeights:
    sems = 14

    def __init__(self, me, grad, first_col, width, inbox, stage, part, left, right, send, recv, load):
        self.me, self.grad, self.width = me, grad, width
        self.cols = (pl.ds(first_col, width), pl.ds(first_col + width, width))
        self.inbox, self.stage, self.part, self.left, self.right = inbox, stage, part, left, right
        self.send, self.recv, self.load = send, recv, load

    def store(self, i, value):
        xlo, z = lax.div(i, 4), lax.rem(i, 4)
        value = value.astype(BF)
        self.grad[rows_at(z * 512 + xlo * 256, 256), self.cols[0]] = value[:, :self.width]
        for c in (0, 1):
            self.grad[rows_at((xlo * 2 + c) * 512 + z * 128, 128), self.cols[1]] = value[
                c * 128:(c + 1) * 128, self.width:]

    def block(self, way, i):
        return self.grad.at[rows_at(i * 512, 512), self.cols[way]]

    def over_x(self, sources, dst, base):
        me = self.me
        for xlo in (0, 1):
            for c in (0, 1):
                src = sources(xlo, c)
                x = me.c * 2 + xlo
                self_too = jnp.logical_and(me.x == x, me.c == c)

                @pl.when(self_too)
                def _():
                    pltpu.make_async_copy(src, dst, self.recv.at[base + me.x]).start()

                @pl.when(jnp.logical_not(self_too))
                def _():
                    remote(src, dst, self.send.at[base + xlo * 2 + c], self.recv.at[base + me.x],
                           me.at(x=x, c=c)).start()

    def over_x_sent(self, ref, base):
        me = self.me
        for xlo in (0, 1):
            for c in (0, 1):
                @pl.when(jnp.logical_or(me.x != me.c * 2 + xlo, me.c != c))
                def _():
                    settle(ref, self.send.at[base + xlo * 2 + c])

    def first(self):
        me = self.me
        for k in (1, 3, 2):
            z = ring(me.z, k)
            remote(self.block(0, z), self.inbox.at[k - 1], self.send.at[k - 1], self.recv.at[k - 1],
                   me.at(z=z)).start()
        self.over_x(lambda xlo, c: self.block(1, xlo * 2 + c), self.inbox.at[3 + me.x], 3)

    def second(self):
        me = self.me
        for i in range(7):
            settle(self.inbox.at[i], self.recv.at[i])
            pltpu.make_async_copy(self.inbox.at[i], self.stage[i], self.load.at[i]).start()
        for i in range(7):
            settle(self.stage[i], self.load.at[i])

        def add_z(i, _):
            rows = pl.ds(pl.multiple_of(i * 32, 32), 32)
            here = pl.ds(pl.multiple_of(me.z * 512 + i * 32, 32), 32)
            total = self.grad[here, self.cols[0]].astype(F32)
            for k in range(3):
                total = total + self.stage[k][rows, :].astype(F32)
            self.grad[here, self.cols[0]] = total.astype(BF)
            total = self.stage[3][rows, :].astype(F32)
            for k in range(4, 7):
                total = total + self.stage[k][rows, :].astype(F32)
            self.part[rows, :] = total.astype(BF)
            return 0

        lax.fori_loop(0, 16, add_z, 0)
        self.over_x(lambda xlo, c: self.grad.at[rows_at(me.z * 512 + xlo * 256 + c * 128, 128), self.cols[0]],
                    self.left.at[me.x], 7)
        for k in (1, 3, 2):
            z = ring(me.z, k)
            remote(self.part.at[rows_at(z * 128, 128)], self.right.at[k - 1], self.send.at[10 + k],
                   self.recv.at[10 + k], me.at(z=z)).start()

    def third(self, store):
        me = self.me
        for i in range(4):
            settle(self.left.at[i], self.recv.at[7 + i])
        for k in (1, 2, 3):
            settle(self.right.at[k - 1], self.recv.at[10 + k])

        def add(i, _):
            rows = pl.ds(pl.multiple_of(i * 32, 32), 32)
            left = self.left[0, rows, :].astype(F32)
            for x in range(1, 4):
                left = left + self.left[x, rows, :].astype(F32)
            right = self.part[pl.ds(pl.multiple_of(me.z * 128 + i * 32, 32), 32), :].astype(F32)
            for k in range(3):
                right = right + self.right[k, rows, :].astype(F32)
            store(rows, left, right)
            return 0

        lax.fori_loop(0, 4, add, 0)

    def finish(self):
        me = self.me
        for k in (1, 2, 3):
            settle(self.inbox.at[k - 1], self.send.at[k - 1])
            settle(self.right.at[k - 1], self.send.at[10 + k])
        self.over_x_sent(self.inbox.at[3], 3)
        self.over_x_sent(self.left.at[0], 7)


def dot_rows(left, right):
    return lax.dot_general(left, right, (((0,), (0,)), ((), ())), preferred_element_type=F32)


def back_norm(values, gain, upstream):
    entries = values.shape[-1]
    inverse = inverse_of(values)
    scaled = upstream * gain
    folded = jnp.sum(scaled * values, axis=-1, keepdims=True)
    grad = inverse * scaled - values * (inverse * inverse * inverse) * folded / entries
    return grad, jnp.sum(upstream * values * inverse, axis=0, keepdims=True)


def backward_kernel(
    tokens, cot, attn_gain, mlp_gain, query_gain, key_gain,
    n_in, cot_in, n2_in, a_in, b_in, qlin_in, klin_in, qrot_in, kv_in, o_in, mid_in, cosine, sine,
    result, tokens_grad, gains_out, qkv_grad, out_grad, gate_grad, up_grad, down_grad, box_q, box_o, box_g, box_u, box_d,
    n2, cota, a, b, da, h, dg, du, qlin, klin, qrot, kv, o, mid, dmid, cos, sin, dqkv, d_o, acc, acc_out, acc_in,
    sib_out, held, arrive, held2, arrive2,
    part_q, left_q, right_q, part_o, left_o, right_o, part_g, left_g, right_g, part_u, left_u, right_u,
    part_d, left_d, right_d, gain8, gainx, gainz,
    load, r1_send, r1_recv, r2_send, r2_recv, r3_send, r3_recv, da_send, da_recv,
    q_send, q_recv, o_send, o_recv, g_send, g_recv, u_send, u_recv, d_send, d_recv, stage_load, swap_sem, v_send, v_recv,
):
    me = Place()
    barrier, count = greet(me, True)
    waits = {}

    def fetch(name, src, dst):
        waits[name] = pltpu.make_async_copy(src, dst, load.at[len(waits)])
        waits[name].start()

    fetch("n2", n2_in, n2)
    fetch("b", b_in, b)
    fetch("cot", cot_in, cota)
    fetch("mid", mid_in, mid)
    fetch("a", a_in, a)
    fetch("o", o_in, o)
    fetch("qrot", qrot_in, qrot)
    fetch("kv", kv_in, kv)
    fetch("qlin", qlin_in, qlin)
    fetch("klin", klin_in, klin)
    fetch("cos", cosine.at[me.xhi], cos)
    fetch("sin", sine.at[me.xhi], sin)
    pl.semaphore_wait(barrier, count)
    waits["n2"].wait()
    waits["b"].wait()
    waits["cot"].wait()

    def hidden(i, _):
        rows = rows_at(lax.div(i, 3) * 512, 512)
        j = lax.rem(i, 3) * 256
        cols = rows_at(j, 256)
        gate = dot(n2[rows, :], b[:, cols])
        up = dot(n2[rows, :], b[:, rows_at(768 + j, 256)])
        d_hidden = dot(cota[rows, :], b[:, rows_at(1536 + j, 256)])
        sg = jax.nn.sigmoid(gate)
        active = gate * sg
        h[rows, cols] = (active * up).astype(BF)
        dg[rows, cols] = (d_hidden * up * sg * (1.0 + gate * (1.0 - sg))).astype(BF)
        du[rows, cols] = (d_hidden * active).astype(BF)
        return 0

    lax.fori_loop(0, 6, hidden, 0)
    sum_n2 = ReduceRows(me, sib_out, held, arrive, r1_send, r1_recv)
    sum_result = ReduceRows(me, sib_out, held2, arrive2, r2_send, r2_recv)
    sum_n = ReduceRows(me, sib_out, held, arrive, r3_send, r3_recv)

    def back_n2(row, j):
        rows, model = rows_at(row, 256), rows_at(j * 512, 512)
        return dot_t(dg[rows, :], b[model, 0:768]) + dot_t(du[rows, :], b[model, 768:1536])

    def down(row, j):
        return dot_t(h[rows_at(row, 256), :], b[rows_at(j * 512, 512), 1536:2304])

    sum_n2.other(back_n2)
    sum_n2.mine(back_n2)
    stage = [buf.at[pl.ds(r * 512, 512), pl.ds(q * 384, 384)] for buf in (dg, du) for r in (0, 1) for q in (0, 1)]
    stage_small = [buf.at[pl.ds(r * 512, 512), pl.ds(q * 384, 256)] for buf in (dg, du) for r in (0, 1) for q in (0, 1)]
    stage_o = [buf.at[pl.ds(r * 512, 512), pl.ds(q * 384, 128)] for buf in (dg, du) for r in (0, 1) for q in (0, 1)]
    red_g = ReduceWeights(me, b, 0, 384, box_g, stage, part_g, left_g, right_g, g_send, g_recv, stage_load)
    red_u = ReduceWeights(me, b, 768, 384, box_u, stage, part_u, left_u, right_u, u_send, u_recv, stage_load)
    red_d = ReduceWeights(me, b, 1536, 384, box_d, stage, part_d, left_d, right_d, d_send, d_recv, stage_load)
    red_o = ReduceWeights(me, a, 512, 128, box_o, stage_o, part_o, left_o, right_o, o_send, o_recv, stage_load)
    red_q = ReduceWeights(me, a, 0, 256, box_q, stage_small, part_q, left_q, right_q, q_send, q_recv, stage_load)

    def weight_grad(red, left, right):
        def step(i, _):
            red.store(i, dot_rows(left[:, rows_at(i * 256, 256)], right[...]))
            return 0

        lax.fori_loop(0, 8, step, 0)
        red.first()

    weight_grad(red_g, n2, dg)
    weight_grad(red_u, n2, du)
    sum_n2.finish()
    sum_result.other(down)
    sum_n2.wait()
    waits["mid"].wait()
    rows_da = GatherRows(me, da, da_send, da_recv)
    own = (me.c * 4 + me.y) * BLOCK

    def back_two(i, total):
        rows = pl.ds(pl.multiple_of(i * 16, 16), 16)
        grad, gain = back_norm(mid[rows, :], mlp_gain[...], sum_n2.total(i * 16))
        grad = grad + cot[rows, :].astype(F32)
        dmid[rows, :] = grad
        da[pl.ds(pl.multiple_of(own + i * 16, 16), 16), :] = grad.astype(BF)
        return total + gain

    mlp_part = lax.fori_loop(0, 8, back_two, jnp.zeros((1, WIDTH), F32))
    rows_da.start()
    slot = me.c * 4 + me.y
    gain8[slot, 1:2, :] = mlp_part
    rows_da.relay()
    sum_result.mine(down)
    weight_grad(red_d, cota, h)
    rows_da.finish()
    n_load = pltpu.make_async_copy(n_in, cota, load.at[12])
    n_load.start()
    for name in ("a", "o", "qrot", "kv", "qlin", "klin", "cos", "sin"):
        waits[name].wait()

    def back_o(i, _):
        rows = rows_at(i * 512, 512)
        d_o[rows, :] = dot(da[rows, :], a[:, 512:768]).astype(BF)
        return 0

    lax.fori_loop(0, 2, back_o, 0)
    weight_grad(red_o, da, o)

    swaps = []
    q_gain = jnp.zeros((1, HEAD), F32)
    for turn_ in (0, 1):
        s = 1 - me.c if turn_ == 0 else me.c
        for block in (3, 2, 1, 0):
            keys = rows_at(s * 512, (block + 1) * 128)
            rows = rows_at(s * 512 + block * 128, 128)
            q = qrot[rows_at(s * 1024 + block * 256, 256), :]
            g = jnp.concatenate([d_o[rows, 0:128], d_o[rows, 128:256]], axis=0)
            shape = (256, (block + 1) * 128)
            row = lax.rem(lax.broadcasted_iota(jnp.int32, shape, 0), 128)
            col = lax.broadcasted_iota(jnp.int32, shape, 1)
            near = jnp.where(col <= row + block * 128, jnp.exp2(dot_t(q, kv[0, keys, :]) * SCORE2), 0.0)
            far = jnp.where(col < (block + me.xhi) * 128, jnp.exp2(dot_t(q, kv[2, keys, :]) * SCORE2), 0.0)
            scale = 1.0 / (jnp.sum(near, axis=-1, keepdims=True) + jnp.sum(far, axis=-1, keepdims=True))
            near, far = near * scale, far * scale
            d_near, d_far = dot_t(g, kv[1, keys, :]), dot_t(g, kv[3, keys, :])
            delta = jnp.sum(d_near * near, axis=-1, keepdims=True) + jnp.sum(d_far * far, axis=-1, keepdims=True)
            s_near, s_far = (near * (d_near - delta)).astype(BF), (far * (d_far - delta)).astype(BF)
            dq = (dot(s_near, kv[0, keys, :]) + dot(s_far, kv[2, keys, :])) * SCORE
            parts = (dot_rows(s_near, q) * SCORE, dot_rows(near.astype(BF), g),
                     dot_rows(s_far, q) * SCORE, dot_rows(far.astype(BF), g))
            for i, value in enumerate(parts):
                if block == 3:
                    acc[i, keys, :] = value
                else:
                    acc[i, keys, :] += value
            turn_rows = pl.ds(block * 128, 128)
            for head in (0, 1):
                up = turn(dq[head * 128:(head + 1) * 128], cos[turn_rows, :], -sin[turn_rows, :])
                grad, gain = back_norm(qlin[rows, head * 128:(head + 1) * 128], query_gain[...], up)
                dqkv[rows, head * 128:(head + 1) * 128] = grad.astype(BF)
                q_gain = q_gain + gain
        rows = rows_at(s * 512, 512)
        for i in (0, 1):
            acc_out[turn_, i] = acc[2 + i, rows, :].astype(BF)
        swap = remote(acc_out.at[turn_], acc_in.at[turn_], swap_sem.at[turn_], swap_sem.at[2 + turn_],
                      me.at(x=ring(me.x, 2)))
        swap.start()
        swaps.append(swap)

    k_gain = jnp.zeros((1, HEAD), F32)

    def back_n(row, j):
        rows, model = rows_at(row, 256), rows_at(j * 512, 512)
        return dot_t(dqkv[rows, 0:256], a[model, 0:256]) + dot_t(dqkv[rows, 256:512], a[model, 256:512])

    for turn_ in (0, 1):
        s = 1 - me.c if turn_ == 0 else me.c
        rows = rows_at(s * 512, 512)
        swaps[turn_].wait()
        dk = acc[0, rows, :] + acc_in[turn_, 0].astype(F32)
        dv = acc[1, rows, :] + acc_in[turn_, 1].astype(F32)
        grad, gain = back_norm(klin[rows, :], key_gain[...], turn(dk, cos[...], -sin[...]))
        k_gain = k_gain + gain
        dqkv[rows, 256:384] = grad.astype(BF)
        dqkv[rows, 384:512] = dv.astype(BF)
        if turn_ == 0:
            sum_result.finish()
            sum_n.other(back_n)
        else:
            sum_n.mine(back_n)
    gain8[slot, 2:3, 0:128] = q_gain
    gain8[slot, 2:3, 128:256] = k_gain
    n_load.wait()
    weight_grad(red_q, cota, dqkv)

    def put(ref):
        def store(rows, left, right):
            width = left.shape[1]
            ref[rows, 0:width] = left
            ref[rows, width:2 * width] = right
        return store

    reds = ((red_g, gate_grad), (red_u, up_grad), (red_d, down_grad), (red_o, out_grad), (red_q, qkv_grad))
    for red, _ in reds[:4]:
        red.second()
    sum_result.wait()

    def finish_result(i, _):
        rows = pl.ds(pl.multiple_of(i * 16, 16), 16)
        result[rows, :] = (mid[rows, :] + sum_result.total(i * 16)).astype(BF)
        return 0

    lax.fori_loop(0, 8, finish_result, 0)
    sum_n.wait()

    def back_one(i, total):
        rows = pl.ds(pl.multiple_of(i * 16, 16), 16)
        grad, gain = back_norm(tokens[rows, :].astype(F32), attn_gain[...], sum_n.total(i * 16))
        tokens_grad[rows, :] = dmid[rows, :] + grad
        return total + gain

    gain8[slot, 0:1, :] = lax.fori_loop(0, 8, back_one, jnp.zeros((1, WIDTH), F32))

    peers = [(me.y, 1 - me.c)] + [(ring(me.y, k), c) for k in (1, 2, 3) for c in (0, 1)]
    for i, (y, c) in enumerate(peers):
        remote(gain8.at[slot], gain8.at[slot], v_send.at[i], v_recv.at[slot], me.at(y=y, c=c)).start()
    red_q.second()
    for i in range(8):
        @pl.when(slot != i)
        def _():
            settle(gain8.at[i], v_recv.at[i])
    total = gain8[0]
    for i in range(1, 8):
        total = total + gain8[i]
    gainx[me.x] = total
    for k in (1, 2, 3):
        remote(gainx.at[me.x], gainx.at[me.x], v_send.at[6 + k], v_recv.at[8 + me.x], me.at(x=ring(me.x, k))).start()
    for red, ref in reds[:3]:
        red.third(put(ref))
    for i in range(4):
        @pl.when(me.x != i)
        def _():
            settle(gainx.at[i], v_recv.at[8 + i])
    gainz[me.z] = gainx[0] + gainx[1] + gainx[2] + gainx[3]
    for k in (1, 2, 3):
        remote(gainz.at[me.z], gainz.at[me.z], v_send.at[9 + k], v_recv.at[12 + me.z], me.at(z=ring(me.z, k))).start()
    for red, ref in reds[3:]:
        red.third(put(ref))
    for i in range(4):
        @pl.when(me.z != i)
        def _():
            settle(gainz.at[i], v_recv.at[12 + i])
    gains_out[...] = gainz[0] + gainz[1] + gainz[2] + gainz[3]
    for i in range(13):
        settle(gain8.at[0], v_send.at[i])
    sum_n.finish()
    for red, _ in reds:
        red.finish()


def backward(tokens, cot, gains, saved, cos, sin):
    n, cota, n2, a, b, qlin, klin, qrot, kv, o, mid = saved
    args = (tokens, cot) + gains + saved + (cos, sin)
    vmem = pl.BlockSpec(memory_space=pltpu.VMEM)
    hbm = pl.BlockSpec(memory_space=pl.ANY)
    outs = [((BLOCK, WIDTH), BF), ((BLOCK, WIDTH), F32), ((8, WIDTH), F32), ((BLOCK, 512), F32), ((BLOCK, 256), F32)]
    outs += [((BLOCK, 768), F32)] * 3
    widths = (256, 128, 384, 384, 384)
    boxes = [((7, 512, w), BF) for w in widths]
    scratch = [
        ((ROWS, WIDTH), BF), ((ROWS, WIDTH), BF), ((WIDTH, A_COLS), BF), ((WIDTH, B_COLS), BF), ((ROWS, WIDTH), BF),
        ((ROWS, 768), BF), ((ROWS, 768), BF), ((ROWS, 768), BF), ((ROWS, 256), F32), ((ROWS, 128), F32),
        ((2 * ROWS, 128), BF), ((4, ROWS, 128), BF), ((ROWS, 256), BF), ((BLOCK, WIDTH), F32), ((BLOCK, WIDTH), F32),
        ((512, 128), F32), ((512, 128), F32), ((ROWS, 512), BF), ((ROWS, 256), BF), ((4, ROWS, 128), F32),
        ((2, 2, 512, 128), BF), ((2, 2, 512, 128), BF),
        ((512, WIDTH), BF), ((512, WIDTH), BF), ((3, BLOCK, WIDTH), BF), ((512, WIDTH), BF), ((3, BLOCK, WIDTH), BF),
    ]
    for w in widths:
        scratch += [((512, w), BF), ((4, BLOCK, w), BF), ((3, BLOCK, w), BF)]
    scratch += [((8, 8, WIDTH), F32), ((4, 8, WIDTH), F32), ((4, 8, WIDTH), F32)]
    scratch = [pltpu.VMEM(s, d) for s, d in scratch]
    dma = pltpu.SemaphoreType.DMA
    scratch += [dma((13,))] + [dma((6,))] * 6 + [dma((8,))] * 2 + [dma((14,))] * 10 + [dma((7,)), dma((4,))]
    scratch += [dma((13,)), dma((16,))]
    got = pl.pallas_call(
        backward_kernel,
        out_shape=[jax.ShapeDtypeStruct(s, d) for s, d in outs + boxes],
        in_specs=[vmem] * 6 + [hbm] * 13,
        out_specs=[vmem] * len(outs) + [hbm] * len(boxes),
        scratch_shapes=scratch,
        compiler_params=pltpu.CompilerParams(
            collective_id=2, has_side_effects=True, vmem_limit_bytes=VMEM_BYTES),
        name="backward_part",
    )(*args)
    return got[:len(outs)]


def local(tokens, cotangent, attn_gain, mlp_gain, query_gain, key_gain, *weights):
    cos, sin = rope_tables()
    gains = (attn_gain[None], mlp_gain[None], query_gain[None], key_gain[None])
    saved = forward(tokens, cotangent, *gains, *weights, cos, sin)
    result, tokens_grad, gains_out, qkv, out, gate, up, down = backward(tokens, cotangent, gains, tuple(saved), cos, sin)
    return (
        result, tokens_grad, gains_out[0], gains_out[1], gains_out[2, 0:128], gains_out[2, 128:256],
        qkv[:, 0:256], qkv[:, 256:384], qkv[:, 384:512], out, gate, up, down,
    )


def solution(mesh):
    rows, plane = P(("dp", "tensor"), None), P("dp", "tensor")
    return jax.shard_map(
        local,
        mesh=mesh,
        in_specs=(rows, rows, P(), P(), P(), P()) + (plane,) * 7,
        out_specs=(rows, rows, P(), P(), P(), P()) + (plane,) * 7,
        check_vma=False,
    )
```

time: 1340 us -> 306 us (0.23)
  waiting for transfers between devices: 994 us -> 0 us
  Pallas kernels: 0 us -> 291 us
  matrix products: 128 us -> 0 us
  blocking collectives: 114 us -> 0 us
  other arithmetic: 46.2 us -> 0 us
  local copies, waits for them, and re-layouts: 33.3 us -> 13 us
  between operations: 15.1 us -> 0.7 us
    reduce_scatter x10 -> x0, waiting for transfers between devices: 652 us -> none  [the longest x1 114 us: local(): lax.psum_scatter(times_transposed(attended, out_full), 'tensor', scatter_...]
    all_gather x9 -> x0, waiting for transfers between devices: 337 us -> none  [the longest x1 74.3 us: local(): lax.all_gather(normed_mlp.astype(jnp.bfloat16), 'tensor', axis=0, tiled=T...]
    pallas_call x0 -> x2, Pallas kernels: none -> 291 us  [the longest x1 169 us: backward(): pl.pallas_call(backward_kernel, out_shape=[jax.ShapeDtypeStruct(s, d) for...]
    dot_general x35 -> x0, matrix products: 128 us -> none  [the longest x7 41.7 us: contract_rows(): lax.dot_general(left, right, (((0,), (0,)), ((), ())), preferred_element_...]
    psum x1 -> x0, blocking collectives: 70.8 us -> none  [local(): lax.psum((attn_gain_part, mlp_gain_part, query_gain_part, key_gain_part),...]
    all_gather x2 -> x0, blocking collectives: 43.1 us -> none  [the longest x1 23.3 us: local(): lax.all_gather(key_weight, 'dp', axis=0, tiled=True)]
    convert_element_type x11 -> x0, other arithmetic: 16.5 us -> none  [the longest x6 9.27 us: local(): query_grad, key_grad, value_grad, out_grad, gate_grad, up_grad, down_grad...]
  transfers between devices with their start and end apart: 20 -> 0, of which waited for: 19 -> 0; matrix products, arithmetic and copies ran while one was open for 12% -> 0% of each run, Pallas kernels for 0% -> 0%
where the time goes in v1:
time: 306 us; the launch traced here: 305 us
  Pallas kernels  291 us (95%)
  local copies, waits for them, and re-layouts  13 us (4%)
    pallas_call x1, Pallas kernels, backward(): pl.pallas_call(backward_kernel, out_shape=[jax.ShapeDtypeStruct(s, d) for...  169 us
    pallas_call x1, Pallas kernels, forward(): pl.pallas_call(forward_kernel, out_shape=[jax.ShapeDtypeStruct(s, d) for...  122 us
    unnamed x14, local copies, waits for them, and re-layouts  7.08 us

profile of v1, /device:TPU:0, one launch (start us, length us, event | category | flops | bytes accessed | tf_op | source)
XLA Modules:
  0.0 304.9 jit_solution(13607471249506766006)
XLA Ops:
  0.6 121.7 %forward_part.1 = (bf16[1024,2048]{1,0:T(8,128)(2,1)}, bf16[1024,2048]{1,0:T(8,128)(2,1)}, bf16[1024,2048]{1,0:T(8,128)(2,1)}, bf16[2048,768]{1,0:T(8,128)(2,1)}...) custom-call(bf16[128,2048]{1,0:T(8,128)(2,1)} %tokens.3, ...), custom_call_target="tpu_custom_call" | custom-call | tf_op jit(solution)/shard_map/forward_part/pallas_call | solution.py:435
  122.4 169.4 %backward_part.1 = (bf16[128,2048]{1,0:T(8,128)(2,1)}, f32[128,2048]{1,0:T(8,128)}, f32[8,2048]{1,0:T(8,128)}, f32[128,512]{1,0:T(8,128)}, f32[128,256]{1,0:T(8,...) custom-call(bf16[128,2048]{1,0:T(8,128)(2,1)} %tokens.3, ...), custom_call_target="tpu_custom_call" | custom-call | tf_op jit(solution)/shard_map/backward_part/pallas_call | solution.py:855
  291.9 0.0 copy-start.3
  291.9 0.0 copy-start.2
  291.9 0.0 copy-start.1
  291.9 0.0 copy-start
  291.9 1.3 slice_bitcast_fusion
  293.2 1.5 fusion.1
  294.7 1.6 slice.25
  296.3 1.5 fusion
  297.8 1.9 copy.34
  299.7 2.3 copy.35
  302.0 0.0 copy-done.3
  302.0 0.7 copy.36
  302.6 0.0 copy-done.2
  302.6 0.7 copy.37
  303.4 0.0 copy-done.1
  303.4 0.7 copy.38
  304.1 0.0 copy-done
  304.1 0.7 copy.39
Async XLA Ops:
  291.9 10.1 %copy-start.3 = (f32[128,256]{1,0:T(8,128)S(1)}, f32[128,256]{1,0:T(8,128)}, u32[]{:S(2)}) copy-start(f32[128,256]{1,0:T(8,128)} %get-tuple-element.79) | copy-start | bytes 393220
  291.9 10.8 %copy-start.2 = (f32[128,768]{1,0:T(8,128)S(1)}, f32[128,768]{1,0:T(8,128)}, u32[]{:S(2)}) copy-start(f32[128,768]{1,0:T(8,128)} %get-tuple-element.80) | copy-start | bytes 1179652
  291.9 11.5 %copy-start.1 = (f32[128,768]{1,0:T(8,128)S(1)}, f32[128,768]{1,0:T(8,128)}, u32[]{:S(2)}) copy-start(f32[128,768]{1,0:T(8,128)} %get-tuple-element.81) | copy-start | bytes 1179652
  291.9 12.3 %copy-start = (f32[128,768]{1,0:T(8,128)S(1)}, f32[128,768]{1,0:T(8,128)}, u32[]{:S(2)}) copy-start(f32[128,768]{1,0:T(8,128)} %get-tuple-element.82) | copy-start | bytes 1179652
